TPU v7x, 512 devices: a whole 4x8x8 slice. The times are simulated.
512 devices in a mesh: dev: 128 (over z, y, core), rep: 4 (over x).
Axes of the slice: x: 4, y: 8, z: 8, core: 2. Of those that a mesh axis runs over, the one named last changes fastest.
Arguments:
- params: float32 [10, 65536], P(None, 'dev'), may hold values from -8 to 6
- moment1: float32 [10, 65536], P(None, 'dev'), may hold values from -0.06 to 0.06
- moment2: float32 [10, 65536], P(None, 'dev'), may hold values from 0.0001 to 0.01
- camera: float32 [4, 8], P('rep'), may hold values from -3 to 3
- owner: int32 [4, 256, 512, 1], P('rep', 'dev'), may hold values from 0 to 127; in each aligned block of 1024 rows (0 to 1023, 1024 to 2047, ..., all dimensions but the last counted through in order) at most 16 rows name the same one
- local_index: int32 [4, 256, 512], P('rep', 'dev'), may hold values from 0 to 511
- target: float32 [4, 256, 3, 256], P('rep', 'dev'), may hold values from 0 to 1
- rehome: int32 [128, 128], P('dev'), may hold values from 0 to 127, each once within a row
Outputs:
- params_next: float32 [10, 65536], P(None, 'dev')
- moment1_next: float32 [10, 65536], P(None, 'dev')
- moment2_next: float32 [10, 65536], P(None, 'dev')
- rendered: float32 [4, 256, 3, 256], P('rep', 'dev')
Inputs may be any that keep to these rules, and one draw needn't show every extreme that they name: In the entries of one device's tiles of one camera (aligned blocks of 1024 entries) no owner is named more than 16 times, a bound that some block reaches. `rehome`: each row is a permutation of the devices.
All inputs are finite; a program needn't handle non-finite values.
Results may differ from a plain program's by a relative error of at most 0.00014.
Values sent between devices are 32-bit elements; how exact they have to be, the bound alone decides.
No kernel may reach another device: no remote copies, remote signals or barrier semaphores. Data moves between devices by JAX's collectives and lax.ppermute only.
A program may use at most 128 MiB of HBM per device.

v0:
```python
import functools
import jax
import jax.numpy as jnp
from jax import lax
from jax.sharding import PartitionSpec as P

SIDE = 16
PIX = 256
BACKGROUND = 0.5


def project(params, camera_row):
    xpos = params[0]
    ypos = params[1]
    zpos = params[2]
    screen_u = camera_row[0] * xpos + camera_row[1] * ypos + camera_row[2] * zpos + camera_row[3]
    screen_v = camera_row[4] * xpos + camera_row[5] * ypos + camera_row[6] * zpos + camera_row[7]
    conic_a = jnp.exp(params[3])
    conic_c = jnp.exp(params[5])
    conic_b = 0.9 * jnp.tanh(params[4]) * jnp.sqrt(conic_a * conic_c)
    opacity = jax.nn.sigmoid(params[6])
    colors = jax.nn.sigmoid(params[7:10])
    head = jnp.stack([screen_u, screen_v, conic_a, conic_b, conic_c, opacity])
    return jnp.concatenate([head, colors], axis=0)


def render(values):
    pixel_ids = jnp.arange(PIX)
    column = (pixel_ids % SIDE).astype(jnp.float32) - 7.5
    row_pos = (pixel_ids // SIDE).astype(jnp.float32) - 7.5
    delta_u = column[None, :, None] - values[:, 0][:, None, :]
    delta_v = row_pos[None, :, None] - values[:, 1][:, None, :]
    quad = (
        values[:, 2][:, None, :] * delta_u * delta_u
        + 2.0 * values[:, 3][:, None, :] * delta_u * delta_v
        + values[:, 4][:, None, :] * delta_v * delta_v
    )
    alpha = 0.99 * values[:, 5][:, None, :] * jnp.exp(-0.5 * quad)
    log_keep = jnp.log(1.0 - alpha)
    running = jnp.cumsum(log_keep, axis=2)
    weight = alpha * jnp.exp(running - log_keep)
    image = jnp.einsum("bpk,bck->bcp", weight, values[:, 6:9], precision=lax.Precision.HIGHEST)
    return image + BACKGROUND * jnp.exp(running[:, :, -1])[:, None, :]


def local(params, moment1, moment2, camera, owner, local_index, target, rehome):
    devices = lax.axis_size("dev")
    gauss_dev = params.shape[1]
    tiles_dev = local_index.shape[1]
    list_len = local_index.shape[2]
    projected, pullback = jax.vjp(functools.partial(project, camera_row=camera[0]), params)
    destination = owner[0, :, :, 0].reshape(-1)
    local_ids = local_index[0].reshape(-1)
    whole = lax.all_gather(projected, "dev", axis=1, tiled=True)
    global_ids = destination * gauss_dev + local_ids
    entries = jnp.take(whole, global_ids, axis=1)
    values = (
        entries.reshape(9, tiles_dev, list_len)
        .transpose(1, 0, 2)
        .reshape(tiles_dev // 2, 2, 9, list_len)
    )
    goals = target[0].reshape(tiles_dev // 2, 2, 3, PIX)

    def one_block(pair):
        block_values, block_target = pair
        image, pull_render = jax.vjp(render, block_values)
        return (image, pull_render(image - block_target)[0])

    images, grad_values = lax.map(one_block, (values, goals))
    grad_entries = grad_values.reshape(tiles_dev, 9, list_len).transpose(1, 0, 2).reshape(9, -1)
    spread = jnp.zeros((9, gauss_dev * devices), jnp.float32).at[:, global_ids].add(grad_entries)
    grad_table = lax.psum_scatter(spread, "dev", scatter_dimension=1, tiled=True)
    grad_local = pullback(grad_table)[0]
    grad_total = lax.psum(grad_local, "rep")
    moment1_new = 0.9 * moment1 + 0.1 * grad_total
    moment2_new = 0.99 * moment2 + 0.01 * grad_total * grad_total
    params_new = params - 0.01 * moment1_new / (jnp.sqrt(moment2_new) + 1e-08)
    stacked = jnp.stack([params_new, moment1_new, moment2_new]).reshape(
        3, 10, devices, gauss_dev // devices
    )
    block_ids = jnp.arange(devices, dtype=jnp.int32)
    matches = (rehome[0][:, None] == block_ids[None, :]).astype(jnp.int32)
    inverse = jnp.sum(matches * block_ids[:, None], axis=0)
    outgoing_blocks = jnp.take(stacked, inverse, axis=2)
    arrived = lax.all_to_all(
        outgoing_blocks, "dev", split_axis=2, concat_axis=2, tiled=True
    ).reshape(3, 10, gauss_dev)
    return (arrived[0], arrived[1], arrived[2], images)


def solution(mesh):
    in_specs = (
        P(None, "dev"),
        P(None, "dev"),
        P(None, "dev"),
        P("rep", None),
        P("rep", "dev", None, None),
        P("rep", "dev", None),
        P("rep", "dev", None, None),
        P("dev", None),
    )
    out_specs = (P(None, "dev"), P(None, "dev"), P(None, "dev"), P("rep", "dev", None, None))
    return jax.shard_map(local, mesh=mesh, in_specs=in_specs, out_specs=out_specs, check_vma=False)
```

profile of v0, /device:TPU:1, one launch (start us, length us, event | category | flops | bytes accessed | tf_op | source)
XLA Modules:
  0.0 469.2 jit_solution(8419153605545001573)
XLA Ops:
  7.2 1.6 fusion.66
  8.9 0.8 add_divide_fusion
  9.6 3.5 add_divide_fusion.1
  13.1 3.5 add_add_fusion
  16.6 2.0 concatenate.4
  18.7 0.7 fusion.47
  19.4 0.7 copy.274
  20.1 0.7 compare_and_fusion
  20.8 88.6 %all-gather.2.cloned.1.call-done = f32[9,65536]{1,0:T(8,128)} async-done(((f32[9,512]{1,0:T(8,128)}), f32[9,65536]{1,0:T(8,128)}) %all-gather.2.cloned.1.call-update) | async-done | bytes 2359312 | tf_op jit(solution)/shard_map/all_gather | solution.py:54
  109.4 16.9 %copy.241 = f32[9,65536]{0,1:T(8,128)} copy(f32[9,65536]{1,0:T(8,128)} %all-gather.2.cloned.1.call-done) | data formatting | bytes 4718592 | tf_op jit(solution)/shard_map/all_gather | solution.py:54
  126.4 13.3 %gather_fusion = f32[1024,9]{1,0:T(8,128)S(1)} fusion(f32[9,65536]{0,1:T(8,128)} %copy.241, s32[1024]{0:T(1024)S(1)} %broadcast_clamp_fusion), kind=kCustom, calls=%fused_computation | custom fusion | bytes 77824 | tf_op jit(solution)/shard_map/jit(_take)/gather | solution.py:56
  139.7 0.2 copy.243
  140.9 1.8 fusion.18
  142.7 0.2 broadcast_add_fusion.1
  142.9 0.6 copy.250
  143.5 0.4 reduce_window_sum.33
  143.9 0.3 multiply_reduce_fusion.1
  144.2 1.7 fusion.63
  145.9 1.4 fusion.39
  147.4 0.2 copy.252
  147.5 0.2 fusion.38
  147.7 2.8 pad_add_fusion
  150.5 0.4 reshape.269
  150.8 0.8 copy.253
  151.6 4.3 fusion.67
  156.0 0.2 broadcast_add_fusion
  156.2 0.6 copy.254
  156.8 0.4 reduce_window_sum.35
  157.2 3.2 fusion.24
  160.7 0.2 copy.256
  160.9 19.2 %scatter_custom_fusion = f32[9,65536]{0,1:T(8,128)} fusion(s32[1024]{0:T(1024)S(1)} %bitcast.99, f32[1024,9]{1,0:T(8,128)S(1)} %copy.256, f32[]{:T(128)} %constant.106.clone.1), kind=kCustom, calls=%fused_computation.3 | custom fusion | flops 9216 | bytes 2359300 | tf_op jit(solution)/shard_map/scatter-add | solution.py:71
  180.1 19.4 %copy.257 = f32[9,65536]{1,0:T(8,128)} copy(f32[9,65536]{0,1:T(8,128)} %scatter_custom_fusion) | data formatting | bytes 4718592 | tf_op jit(solution)/shard_map/scatter-add | solution.py:71
  199.7 193.3 %reduce-scatter.2.cloned.1.call-done = f32[9,512]{1,0:T(8,128)} async-done(((f32[9,65536]{1,0:T(8,128)}), f32[9,512]{1,0:T(8,128)}) %reduce-scatter.2.cloned.1.call-update) | async-done | bytes 18448 | tf_op jit(solution)/shard_map/reduce_scatter | solution.py:72
  393.0 4.7 fusion.48
  397.7 0.8 fusion.46
  398.4 0.8 multiply_multiply_fusion.4
  399.3 13.2 %psum.7 = f32[10,512]{1,0:T(8,128)S(1)} all-reduce(f32[10,512]{1,0:T(8,128)S(1)} %pad_add_fusion.1), channel_id=1, replica_groups=mesh['dev'=128,'rep'=4] {'rep'}, use_global_device_ids=true, to_apply=%region_14.15 | all-reduce | flops 5120 | bytes 40960 | tf_op jit(solution)/shard_map/psum | solution.py:74
  412.8 0.1 copy.259
  412.9 0.1 copy.260
  413.1 0.2 pad_maximum_fusion
  413.3 1.1 gather_fusion.1
  414.4 1.1 select_bitcast_fusion
  415.6 18.6 %all-to-all-start = ((f32[3,10,128,4]{1,3,0,2:T(4,128)}), f32[3,10,128,4]{1,3,0,2:T(4,128)S(1)}, u32[]{:S(2)}, u32[]{:S(2)}) async-start(f32[3,10,128,4]{1,3,0,2:T(4,128)} %select_bitcast_fusion), calls=%async_computation.1 | async-start | bytes 1572864 | tf_op jit(solution)/shard_map/all_to_all | solution.py:85
  434.1 0.6 copy.264
  434.7 25.3 %all-to-all-done = f32[3,10,128,4]{1,3,0,2:T(4,128)S(1)} async-done(((f32[3,10,128,4]{1,3,0,2:T(4,128)}), f32[3,10,128,4]{1,3,0,2:T(4,128)S(1)}, u32[]{:S(2)}, u32[]{:S(2)}) %all-to-all-start) | async-done | bytes 61472 | tf_op jit(solution)/shard_map/all_to_all | solution.py:85
  460.2 0.7 copy.261
  460.9 0.7 copy.262
  461.7 0.7 copy.263
  (58 shorter events, 1.8 us)
Async XLA Ops:
  7.2 137.0 %copy-start.3 = (f32[1,2,3,256]{3,1,2,0:T(2,128)S(1)}, f32[1,2,3,256]{3,1,2,0:T(2,128)}, u32[]{:S(2)}) copy-start(f32[1,2,3,256]{3,1,2,0:T(2,128)} %param.14) | copy-start | bytes 18436
  7.2 102.3 %all-gather.2.cloned.1.call-start = ((), (), s32[]{:S(2)}) async-start(), calls=%async_computation.2 | async-start | bytes 4227072 | tf_op jit(solution)/shard_map/all_gather | solution.py:54
  18.6 374.3 %reduce-scatter.2.cloned.1.call-start = ((), (), s32[]{:S(2)}) async-start(), calls=%async_computation.3 | async-start | bytes 4227072 | tf_op jit(solution)/shard_map/reduce_scatter | solution.py:72
  160.9 38.7 %copy-start.4 = (s32[1,128]{1,0:T(1,128)S(1)}, s32[1,128]{1,0:T(1,128)}, u32[]{:S(2)}) copy-start(s32[1,128]{1,0:T(1,128)} %param.15) | copy-start | bytes 1540
  160.9 232.1 %copy-start = (f32[10,512]{1,0:T(8,128)S(1)}, f32[10,512]{1,0:T(8,128)}, u32[]{:S(2)}) copy-start(f32[10,512]{1,0:T(8,128)} %param.8) | copy-start | bytes 61444
  160.9 251.7 %copy-start.1 = (f32[10,512]{1,0:T(8,128)S(1)}, f32[10,512]{1,0:T(8,128)}, u32[]{:S(2)}) copy-start(f32[10,512]{1,0:T(8,128)} %param.9) | copy-start | bytes 61444
  160.9 251.7 %copy-start.2 = (f32[10,512]{1,0:T(8,128)S(1)}, f32[10,512]{1,0:T(8,128)}, u32[]{:S(2)}) copy-start(f32[10,512]{1,0:T(8,128)} %param.10) | copy-start | bytes 61444
  415.6 44.5 %all-to-all-start = ((f32[3,10,128,4]{1,3,0,2:T(4,128)}), f32[3,10,128,4]{1,3,0,2:T(4,128)S(1)}, u32[]{:S(2)}, u32[]{:S(2)}) async-start(f32[3,10,128,4]{1,3,0,2:T(4,128)} %select_bitcast_fusion), calls=%async_computation.1 | async-start | bytes 1572864 | tf_op jit(solution)/shard_map/all_to_all | solution.py:85
Sparse Core Ops, SparseCore 0:
  18.8 90.6 all-gather.1
  199.7 193.2 reduce-scatter.1
where the time goes:
time: 471 us; the launch traced here: 469 us
  waiting for transfers between devices  307 us (65%)
  local copies, waits for them, and re-layouts  63.2 us (13%)
  other arithmetic  46.4 us (10%)
  starting transfers between devices  18.6 us (4%)
  between operations  14.6 us (3%)
  blocking collectives  13.2 us (3%)
  matrix products  5.91 us (1%)
    reduce_scatter x1, waiting for transfers between devices, local(): lax.psum_scatter(spread, 'dev', scatter_dimension=1, tiled=True)  193 us
    all_gather x1, waiting for transfers between devices, local(): whole = lax.all_gather(projected, 'dev', axis=1, tiled=True)  88.6 us
    all_to_all x1, waiting for transfers between devices, local(): lax.all_to_all(outgoing_blocks, 'dev', split_axis=2, concat_axis=2, tiled...  25.3 us
    scatter-add x1, local copies, waits for them, and re-layouts, local(): jnp.zeros((9, gauss_dev * devices), jnp.float32).at[:, global_ids]  19.4 us
    scatter-add x1, other arithmetic, local(): jnp.zeros((9, gauss_dev * devices), jnp.float32).at[:, global_ids]  19.2 us
    all_to_all x1, starting transfers between devices, local(): lax.all_to_all(outgoing_blocks, 'dev', split_axis=2, concat_axis=2, tiled...  18.6 us
    all_gather x1, local copies, waits for them, and re-layouts, local(): whole = lax.all_gather(projected, 'dev', axis=1, tiled=True)  16.9 us
    gather x2, local copies, waits for them, and re-layouts, local(): entries = jnp.take(whole, global_ids, axis=1)  13.5 us
  transfers between devices with their start and end apart: 3, of which 3 were waited for; matrix products, arithmetic and copies ran while one was open for 1% of the time, Pallas kernels for 0%

commit v1 on v0

--- a/solution.py
+++ b/solution.py
@@ -51,7 +51,9 @@
     projected, pullback = jax.vjp(functools.partial(project, camera_row=camera[0]), params)
     destination = owner[0, :, :, 0].reshape(-1)
     local_ids = local_index[0].reshape(-1)
-    whole = lax.all_gather(projected, "dev", axis=1, tiled=True)
+    whole = jnp.concatenate(
+        lax.all_to_all(jnp.stack([projected] * lax.axis_size("dev")), "dev", 0, 0), axis=1
+    )
     global_ids = destination * gauss_dev + local_ids
     entries = jnp.take(whole, global_ids, axis=1)
     values = (

time: 471 us -> 503 us (1.068)
  starting transfers between devices: 18.6 us -> 37.5 us
  waiting for transfers between devices: 307 us -> 320 us
    all_to_all x0 -> x1, waiting for transfers between devices: none -> 94.3 us  [local(): lax.all_to_all(jnp.stack([projected] * lax.axis_size('dev')), 'dev', 0, 0)]
    all_gather x1 -> x0, waiting for transfers between devices: 88.6 us -> none  [local(): whole = lax.all_gather(projected, 'dev', axis=1, tiled=True)]
    all_to_all x0 -> x1, starting transfers between devices: none -> 18.9 us  [local(): lax.all_to_all(jnp.stack([projected] * lax.axis_size('dev')), 'dev', 0, 0)]
    reshape x0 -> x1, local copies, waits for them, and re-layouts: none -> 17 us  [local(): jnp.concatenate(lax.all_to_all(jnp.stack([projected] * lax.axis_size('dev...]
    all_gather x1 -> x0, local copies, waits for them, and re-layouts: 16.9 us -> none  [local(): whole = lax.all_gather(projected, 'dev', axis=1, tiled=True)]
    reduce_scatter x1, waiting for transfers between devices: 193 us -> 200 us  [local(): lax.psum_scatter(spread, 'dev', scatter_dimension=1, tiled=True)]
where the time goes in v1:
time: 503 us; the launch traced here: 501 us
  waiting for transfers between devices  320 us (64%)
  local copies, waits for them, and re-layouts  63.8 us (13%)
  other arithmetic  46.4 us (9%)
  starting transfers between devices  37.5 us (7%)
  between operations  14.6 us (3%)
  blocking collectives  13.3 us (3%)
  matrix products  5.91 us (1%)
    reduce_scatter x1, waiting for transfers between devices, local(): lax.psum_scatter(spread, 'dev', scatter_dimension=1, tiled=True)  200 us
    all_to_all x1, waiting for transfers between devices, local(): lax.all_to_all(jnp.stack([projected] * lax.axis_size('dev')), 'dev', 0, 0)  94.3 us
    all_to_all x1, waiting for transfers between devices, local(): lax.all_to_all(outgoing_blocks, 'dev', split_axis=2, concat_axis=2, tiled...  25.3 us
    scatter-add x1, local copies, waits for them, and re-layouts, local(): jnp.zeros((9, gauss_dev * devices), jnp.float32).at[:, global_ids]  19.4 us
    scatter-add x1, other arithmetic, local(): jnp.zeros((9, gauss_dev * devices), jnp.float32).at[:, global_ids]  19.2 us
    all_to_all x1, starting transfers between devices, local(): lax.all_to_all(jnp.stack([projected] * lax.axis_size('dev')), 'dev', 0, 0)  18.9 us
    all_to_all x1, starting transfers between devices, local(): lax.all_to_all(outgoing_blocks, 'dev', split_axis=2, concat_axis=2, tiled...  18.6 us
    reshape x1, local copies, waits for them, and re-layouts, local(): jnp.concatenate(lax.all_to_all(jnp.stack([projected] * lax.axis_size('dev...  17 us
  transfers between devices with their start and end apart: 3, of which 3 were waited for; matrix products, arithmetic and copies ran while one was open for 1% of the time, Pallas kernels for 0%

profile of v1, /device:TPU:1, one launch (start us, length us, event | category | flops | bytes accessed | tf_op | source)
XLA Modules:
  0.0 501.0 jit_solution(238114020972739222)
XLA Ops:
  7.2 1.6 fusion.66
  8.8 0.8 add_divide_fusion
  9.6 3.5 add_divide_fusion.1
  13.1 3.5 add_add_fusion
  16.7 2.5 stack.10
  19.1 18.9 %all-to-all-start = ((f32[128,9,512]{2,1,0:T(8,128)}), f32[128,9,512]{2,1,0:T(8,128)}, u32[]{:S(2)}, u32[]{:S(2)}) async-start(f32[128,9,512]{2,1,0:T(8,128)} %stack.10), calls=%async_computation | async-start | bytes 8388608 | tf_op jit(solution)/shard_map/all_to_all | solution.py:55
  38.1 0.7 fusion.47
  38.8 0.7 copy.278
  39.5 0.7 compare_and_fusion
  40.2 94.3 %all-to-all-done = f32[128,9,512]{2,1,0:T(8,128)} async-done(((f32[128,9,512]{2,1,0:T(8,128)}), f32[128,9,512]{2,1,0:T(8,128)}, u32[]{:S(2)}, u32[]{:S(2)}) %all-to-all-start) | async-done | bytes 2359328 | tf_op jit(solution)/shard_map/all_to_all | solution.py:55
  134.6 17.0 %copy.245 = f32[9,128,512]{0,2,1:T(8,128)} copy(f32[9,128,512]{2,0,1:T(8,128)} %bitcast.12) | data formatting | bytes 4718592 | tf_op jit(solution)/shard_map/reshape | solution.py:54
  151.5 13.3 %gather_fusion = f32[1024,9]{1,0:T(8,128)S(1)} fusion(f32[9,65536]{0,1:T(8,128)} %bitcast.85, s32[1024]{0:T(1024)S(1)} %broadcast_clamp_fusion), kind=kCustom, calls=%fused_computation | custom fusion | bytes 77824 | tf_op jit(solution)/shard_map/jit(_take)/gather | solution.py:58
  164.9 0.2 copy.247
  166.0 1.8 fusion.18
  167.9 0.2 broadcast_add_fusion.1
  168.1 0.6 copy.254
  168.7 0.4 reduce_window_sum.33
  169.1 0.3 multiply_reduce_fusion.1
  169.4 1.7 fusion.63
  171.1 1.4 fusion.39
  172.5 0.2 copy.256
  172.7 0.2 fusion.38
  172.8 2.8 pad_add_fusion
  175.6 0.4 reshape.279
  176.0 0.8 copy.257
  176.7 4.3 fusion.67
  181.1 0.2 broadcast_add_fusion
  181.3 0.6 copy.258
  181.9 0.4 reduce_window_sum.35
  182.3 3.2 fusion.24
  185.8 0.2 copy.260
  186.1 19.2 %scatter_custom_fusion = f32[9,65536]{0,1:T(8,128)} fusion(s32[1024]{0:T(1024)S(1)} %bitcast.102, f32[1024,9]{1,0:T(8,128)S(1)} %copy.260, f32[]{:T(128)} %constant.106.clone.1), kind=kCustom, calls=%fused_computation.3 | custom fusion | flops 9216 | bytes 2359300 | tf_op jit(solution)/shard_map/scatter-add | solution.py:73
  205.3 19.4 %copy.261 = f32[9,65536]{1,0:T(8,128)} copy(f32[9,65536]{0,1:T(8,128)} %scatter_custom_fusion) | data formatting | bytes 4718592 | tf_op jit(solution)/shard_map/scatter-add | solution.py:73
  224.8 199.9 %reduce-scatter.2.cloned.1.call-done = f32[9,512]{1,0:T(8,128)} async-done(((f32[9,65536]{1,0:T(8,128)}), f32[9,512]{1,0:T(8,128)}) %reduce-scatter.2.cloned.1.call-update) | async-done | bytes 18448 | tf_op jit(solution)/shard_map/reduce_scatter | solution.py:74
  424.7 4.7 fusion.48
  429.4 0.8 fusion.46
  430.2 0.8 multiply_multiply_fusion.4
  431.1 13.3 %psum.7 = f32[10,512]{1,0:T(8,128)S(1)} all-reduce(f32[10,512]{1,0:T(8,128)S(1)} %pad_add_fusion.1), channel_id=1, replica_groups=mesh['dev'=128,'rep'=4] {'rep'}, use_global_device_ids=true, to_apply=%region_14.15 | all-reduce | flops 5120 | bytes 40960 | tf_op jit(solution)/shard_map/psum | solution.py:76
  444.7 0.1 copy.264
  444.8 0.2 pad_maximum_fusion
  445.1 1.1 gather_fusion.1
  446.2 1.1 select_bitcast_fusion
  447.3 18.6 %all-to-all-start.1 = ((f32[3,10,128,4]{1,3,0,2:T(4,128)}), f32[3,10,128,4]{1,3,0,2:T(4,128)S(1)}, u32[]{:S(2)}, u32[]{:S(2)}) async-start(f32[3,10,128,4]{1,3,0,2:T(4,128)} %select_bitcast_fusion), calls=%async_computation.2 | async-start | bytes 1572864 | tf_op jit(solution)/shard_map/all_to_all | solution.py:87
  465.9 0.6 copy.268
  466.5 25.3 %all-to-all-done.1 = f32[3,10,128,4]{1,3,0,2:T(4,128)S(1)} async-done(((f32[3,10,128,4]{1,3,0,2:T(4,128)}), f32[3,10,128,4]{1,3,0,2:T(4,128)S(1)}, u32[]{:S(2)}, u32[]{:S(2)}) %all-to-all-start.1) | async-done | bytes 61472 | tf_op jit(solution)/shard_map/all_to_all | solution.py:87
  492.0 0.7 copy.265
  492.7 0.7 copy.266
  493.5 0.7 copy.267
  (58 shorter events, 2.0 us)
Async XLA Ops:
  7.2 162.2 %copy-start.3 = (f32[1,2,3,256]{3,1,2,0:T(2,128)S(1)}, f32[1,2,3,256]{3,1,2,0:T(2,128)}, u32[]{:S(2)}) copy-start(f32[1,2,3,256]{3,1,2,0:T(2,128)} %param.14) | copy-start | bytes 18436
  19.1 115.4 %all-to-all-start = ((f32[128,9,512]{2,1,0:T(8,128)}), f32[128,9,512]{2,1,0:T(8,128)}, u32[]{:S(2)}, u32[]{:S(2)}) async-start(f32[128,9,512]{2,1,0:T(8,128)} %stack.10), calls=%async_computation | async-start | bytes 8388608 | tf_op jit(solution)/shard_map/all_to_all | solution.py:55
  38.0 386.7 %reduce-scatter.2.cloned.1.call-start = ((), (), s32[]{:S(2)}) async-start(), calls=%async_computation.3 | async-start | bytes 4227072 | tf_op jit(solution)/shard_map/reduce_scatter | solution.py:74
  186.0 38.7 %copy-start.4 = (s32[1,128]{1,0:T(1,128)S(1)}, s32[1,128]{1,0:T(1,128)}, u32[]{:S(2)}) copy-start(s32[1,128]{1,0:T(1,128)} %param.15) | copy-start | bytes 1540
  186.0 238.7 %copy-start = (f32[10,512]{1,0:T(8,128)S(1)}, f32[10,512]{1,0:T(8,128)}, u32[]{:S(2)}) copy-start(f32[10,512]{1,0:T(8,128)} %param.8) | copy-start | bytes 61444
  186.0 258.3 %copy-start.1 = (f32[10,512]{1,0:T(8,128)S(1)}, f32[10,512]{1,0:T(8,128)}, u32[]{:S(2)}) copy-start(f32[10,512]{1,0:T(8,128)} %param.9) | copy-start | bytes 61444
  186.1 258.3 %copy-start.2 = (f32[10,512]{1,0:T(8,128)S(1)}, f32[10,512]{1,0:T(8,128)}, u32[]{:S(2)}) copy-start(f32[10,512]{1,0:T(8,128)} %param.10) | copy-start | bytes 61444
  447.3 44.5 %all-to-all-start.1 = ((f32[3,10,128,4]{1,3,0,2:T(4,128)}), f32[3,10,128,4]{1,3,0,2:T(4,128)S(1)}, u32[]{:S(2)}, u32[]{:S(2)}) async-start(f32[3,10,128,4]{1,3,0,2:T(4,128)} %select_bitcast_fusion), calls=%async_computation.2 | async-start | bytes 1572864 | tf_op jit(solution)/shard_map/all_to_all | solution.py:87
Sparse Core Ops, SparseCore 0:
  224.8 199.8 reduce-scatter.1
